TPU v7x, 32 devices: a whole 2x2x4 slice. The times are simulated.
32 devices in a mesh: groups: 2 (over y), inner: 2 (over x), outer: 4 (over z), pair: 2 (over core).
Axes of the slice: x: 2, y: 2, z: 4, core: 2. Of those that a mesh axis runs over, the one named last changes fastest.
Arguments:
- tokens: bfloat16 [32, 128, 4096], P(('groups', 'inner', 'outer', 'pair')), parts along dimension 0, may hold values from -6 to 6
- queries: bfloat16 [32, 128, 2048], P(('groups', 'inner', 'outer', 'pair')), parts along dimension 0, may hold values from -54 to 54
- keys: bfloat16 [32, 128, 512], P(('groups', 'inner', 'outer', 'pair')), parts along dimension 0, may hold values from -18 to 18
- grad_out: bfloat16 [32, 128, 2048], P(('groups', 'inner', 'outer', 'pair')), parts along dimension 0, may hold values from -6 to 6
- segment_ids: int32 [32, 128], P(('groups', 'inner', 'outer', 'pair')), parts along dimension 0, may hold values from 0 to 7, never falling along the last dimension, each value on 1 to 32 neighbouring positions
- levels: bfloat16 [4096, 512], P('inner'), may hold values from -127 to 127
- scales: bfloat16 [32, 512], P('inner'), may hold values from 0.00010919571 to 0.00043678284
Outputs:
- attn_out: bfloat16 [32, 128, 2048], P(('groups', 'inner', 'outer', 'pair')), parts along dimension 0
- grad_tokens: bfloat16 [32, 128, 4096], P(('groups', 'inner', 'outer', 'pair')), parts along dimension 0
- grad_weight: float32 [8192, 512], P(('groups', 'inner', 'outer', 'pair')), parts along dimension 0
There are 2 independent parts, one for each index of `groups`. A program takes and returns all parts, laid end to end along the dimension named above; an argument that names none is the same for every part. Nothing has to cross between parts.
Inputs may be any that keep to these rules, and one draw needn't show every extreme that they name: `segment_ids`: within a sequence segment numbers never fall, and each of the 8 segments spans 1 to 32 tokens.
All inputs are finite; a program needn't handle non-finite values.
Results may differ from a plain program's by a relative error of at most 0.0063.
Values may be sent and summed in bfloat16 or wider, within the bound.
A program may use at most 64 MiB of HBM per device.

v0:
```python
import math

import jax
import jax.numpy as jnp
from jax import lax
from jax.sharding import PartitionSpec as P

HD = 128
KVH = 4
GROUP = 4


def dequantize(level_blocks, scale_rows):
    scaled = level_blocks.astype(jnp.float32) * scale_rows.astype(jnp.float32)[:, None, :]
    return scaled.reshape(-1, level_blocks.shape[2]).astype(jnp.bfloat16)


def shards(tokens, queries, keys, grad_out, segment_ids, levels, scales):
    token_rows = tokens[0]
    query_rows = queries[0]
    key_rows = keys[0]
    cotangent = grad_out[0]
    segments = segment_ids[0]
    length = token_rows.shape[0]
    kv_width = levels.shape[1]
    level_blocks = levels.reshape(levels.shape[0] // 128, 128, kv_width)
    query_heads = query_rows.reshape(length, KVH, GROUP, HD)
    key_heads = key_rows.reshape(length, KVH, HD)
    scores = jnp.einsum(
        "ikgd,jkd->kgij", query_heads, key_heads, preferred_element_type=jnp.float32
    ) / math.sqrt(HD)
    positions = jnp.arange(length)
    allowed = (positions[None, :] <= positions[:, None]) & (segments[:, None] == segments[None, :])
    scores = jnp.where(allowed, scores, jnp.float32(-1e30))
    row_max = jnp.max(scores, axis=-1, keepdims=True)
    expo = jnp.exp(scores - row_max)
    attention_p = (expo / jnp.sum(expo, axis=-1, keepdims=True)).astype(jnp.bfloat16)
    grad_heads = cotangent.reshape(length, KVH, GROUP, HD)
    grad_values = jnp.einsum(
        "kgij,ikgd->jkd", attention_p, grad_heads, preferred_element_type=jnp.float32
    )
    grad_values = grad_values.reshape(length, kv_width).astype(jnp.bfloat16)
    piece_levels = lax.all_gather(level_blocks, "inner", axis=0, tiled=True)
    piece_scales = lax.all_gather(scales, "inner", axis=0, tiled=True)
    values = jnp.dot(
        token_rows, dequantize(piece_levels, piece_scales), preferred_element_type=jnp.float32
    ).astype(jnp.bfloat16)
    piece_levels, piece_scales = lax.all_gather((level_blocks, scales), "inner", axis=0, tiled=True)
    piece_weight = dequantize(piece_levels, piece_scales)
    grad_rows = lax.dot_general(
        grad_values, piece_weight, (((1,), (1,)), ((), ())), preferred_element_type=jnp.float32
    ).astype(jnp.bfloat16)
    value_heads = values.reshape(length, KVH, HD)
    output = jnp.einsum(
        "kgij,jkd->ikgd", attention_p, value_heads, preferred_element_type=jnp.float32
    )
    output = output.reshape(length, query_rows.shape[1]).astype(jnp.bfloat16)
    partial_value = lax.dot_general(
        token_rows, grad_values, (((0,), (0,)), ((), ())), preferred_element_type=jnp.float32
    ).astype(jnp.bfloat16)
    inner_count = lax.axis_size("inner")
    outer_count = lax.axis_size(("outer", "pair"))
    term_blocks = partial_value.reshape(inner_count, outer_count, -1, kv_width)
    received = lax.all_to_all(
        term_blocks, ("outer", "pair"), split_axis=1, concat_axis=1, tiled=True
    )
    first_sums = jnp.sum(received.astype(jnp.float32), axis=1)
    received_sums = lax.all_to_all(first_sums, "inner", split_axis=0, concat_axis=0, tiled=True)
    grad_weight = jnp.sum(received_sums, axis=0)
    return (output[None], grad_rows[None], grad_weight)


def solution(mesh):
    return jax.shard_map(
        shards,
        mesh=mesh,
        in_specs=(
            P(("groups", "inner", "outer", "pair"), None, None),
            P(("groups", "inner", "outer", "pair"), None, None),
            P(("groups", "inner", "outer", "pair"), None, None),
            P(("groups", "inner", "outer", "pair"), None, None),
            P(("groups", "inner", "outer", "pair"), None),
            P("inner", None),
            P("inner", None),
        ),
        out_specs=(
            P(("groups", "inner", "outer", "pair"), None, None),
            P(("groups", "inner", "outer", "pair"), None, None),
            P(("groups", "inner", "outer", "pair"), None),
        ),
        check_vma=False,
    )
```

profile of v0, /device:TPU:1, one launch (start us, length us, event | category | flops | bytes accessed | tf_op | source)
XLA Modules:
  0.0 160.2 jit_solution(14861945125343853276)
XLA Ops:
  7.2 0.8 fusion.11
  8.0 0.9 reshape_squeeze.9
  9.0 1.4 reshape_squeeze.10
  10.4 1.3 copy.54
  12.9 1.2 convolution_convert_fusion
  14.2 1.4 copy.58
  15.6 5.2 %copy.40 = bf16[2,8,256,512]{2,0,3,1:T(2,128)(2,1)} copy(bf16[2,8,256,512]{2,1,0,3:T(8,128)(2,1)S(1)} %bitcast.63) | data formatting | bytes 8388608 | tf_op jit(solution)/shard_map/reshape | solution.py:63
  20.8 6.5 %all-to-all-start = ((bf16[2,8,256,512]{2,0,3,1:T(2,128)(2,1)}), bf16[2,8,256,512]{2,0,3,1:T(2,128)(2,1)}, u32[]{:S(2)}, u32[]{:S(2)}) async-start(bf16[2,8,256,512]{2,0,3,1:T(2,128)(2,1)} %copy.40), calls=%async_computation | async-start | bytes 8388608 | tf_op jit(solution)/shard_map/all_to_all | solution.py:64
  27.3 0.7 all-gather.2.cloned.1.call-update
  28.0 3.7 %all_gather.9 = bf16[32,512]{1,0:T(8,128)(2,1)S(1)} all-gather(bf16[16,512]{1,0:T(8,128)(2,1)S(1)} %copy-done.2), channel_id=1, replica_groups=mesh['groups'=2,'inner'=2,'outer'=4,'pair'=2] {'inner'}, dimensions={0}, use_global_device_ids=true | all-gather | bytes 49152 | tf_op jit(solution)/shard_map/all_gather | solution.py:44
  31.7 55.6 %all-gather.2.cloned.1.call-done = bf16[32,128,512]{2,1,0:T(8,128)(2,1)} async-done(((bf16[16,128,512]{2,1,0:T(8,128)(2,1)}), bf16[32,128,512]{2,1,0:T(8,128)(2,1)}) %all-gather.2.cloned.1.call-update) | async-done | bytes 4194320 | tf_op jit(solution)/shard_map/all_gather | solution.py:43
  87.3 3.2 %multiply_convert_fusion = bf16[32,128,512]{2,1,0:T(8,128)(2,1)S(1)} fusion(bf16[32,128,512]{2,1,0:T(8,128)(2,1)} %all-gather.2.cloned.1.call-done, f32[32,512]{1,0:T(8,128)S(1)} %convert_element_type.64), kind=kLoop, calls=%fused_computation.2 | loop fusion | flops 6291456 | bytes 8454144 | tf_op jit(solution)/shard_map/convert_element_type | solution.py:15
  90.5 2.0 %copy-done.1 = bf16[32,128,512]{2,1,0:T(8,128)(2,1)} copy-done((bf16[32,128,512]{2,1,0:T(8,128)(2,1)}, bf16[32,128,512]{2,1,0:T(8,128)(2,1)S(1)}, u32[]{:S(2)}) %copy-start.1) | copy-done | bytes 4194328
  92.5 1.3 convolution_convert_fusion.3
  93.8 26.7 %all-to-all-done = bf16[2,8,256,512]{2,0,3,1:T(2,128)(2,1)} async-done(((bf16[2,8,256,512]{2,0,3,1:T(2,128)(2,1)}), bf16[2,8,256,512]{2,0,3,1:T(2,128)(2,1)}, u32[]{:S(2)}, u32[]{:S(2)}) %all-to-all-start) | async-done | bytes 4194336 | tf_op jit(solution)/shard_map/all_to_all | solution.py:64
  120.5 11.1 %copy.41 = bf16[2,8,256,512]{3,2,1,0:T(8,128)(2,1)} copy(bf16[2,8,256,512]{2,0,3,1:T(2,128)(2,1)} %all-to-all-done) | data formatting | bytes 8388608 | tf_op jit(solution)/shard_map/all_to_all | solution.py:64
  131.7 2.9 %convert_reduce_fusion = f32[2,256,512]{2,1,0:T(8,128)S(1)} fusion(bf16[2,8,256,512]{3,2,1,0:T(8,128)(2,1)} %copy.41), kind=kLoop, calls=%fused_computation.1 | loop fusion | flops 3932160 | bytes 5242880 | tf_op jit(solution)/shard_map/reduce_sum | solution.py:67
  134.5 1.3 copy.43
  135.9 3.6 %all-to-all-start.1 = ((f32[2,256,512]{1,2,0:T(8,128)}), f32[2,256,512]{1,2,0:T(8,128)S(1)}, u32[]{:S(2)}, u32[]{:S(2)}) async-start(f32[2,256,512]{1,2,0:T(8,128)} %copy.43), calls=%async_computation.1 | async-start | bytes 2097152 | tf_op jit(solution)/shard_map/all_to_all | solution.py:68
  139.5 1.4 convolution_convert_fusion.2
  140.8 1.0 copy.45
  141.9 4.6 %fusion.1 = bf16[1,128,4096]{2,1,0:T(8,128)(2,1)} fusion(bf16[128,512]{0,1:T(8,128)(2,1)S(1)} %bitcast.66, bf16[4096,512]{1,0:T(8,128)(2,1)} %bitcast.62), kind=kOutput, calls=%fused_computation.5 | convolution fusion | flops 537395200 | bytes 5373952 | tf_op jit(solution)/shard_map/dot_general | solution.py:50
  146.5 5.7 %all-to-all-done.1 = f32[2,256,512]{1,2,0:T(8,128)S(1)} async-done(((f32[2,256,512]{1,2,0:T(8,128)}), f32[2,256,512]{1,2,0:T(8,128)S(1)}, u32[]{:S(2)}, u32[]{:S(2)}) %all-to-all-start.1) | async-done | bytes 1048608 | tf_op jit(solution)/shard_map/all_to_all | solution.py:68
  152.3 1.0 copy.46
  (12 shorter events, 1.3 us)
Async XLA Ops:
  7.2 5.7 %copy-start = (bf16[1,128,4096]{2,1,0:T(8,128)(2,1)S(1)}, bf16[1,128,4096]{2,1,0:T(8,128)(2,1)}, u32[]{:S(2)}) copy-start(bf16[1,128,4096]{2,1,0:T(8,128)(2,1)} %param.7) | copy-start | bytes 3145732
  12.2 1.9 %copy-start.3 = (f32[4,4,128]{2,1,0:T(4,128)}, f32[4,4,128]{2,1,0:T(4,128)S(1)}, u32[]{:S(2)}) copy-start(f32[4,4,128]{2,1,0:T(4,128)S(1)} %fusion.39) | copy-start | bytes 24580
  20.8 7.2 %copy-start.2 = (bf16[16,512]{1,0:T(8,128)(2,1)S(1)}, bf16[16,512]{1,0:T(8,128)(2,1)}, u32[]{:S(2)}) copy-start(bf16[16,512]{1,0:T(8,128)(2,1)} %param.13) | copy-start | bytes 49156
  20.8 99.8 %all-to-all-start = ((bf16[2,8,256,512]{2,0,3,1:T(2,128)(2,1)}), bf16[2,8,256,512]{2,0,3,1:T(2,128)(2,1)}, u32[]{:S(2)}, u32[]{:S(2)}) async-start(bf16[2,8,256,512]{2,0,3,1:T(2,128)(2,1)} %copy.40), calls=%async_computation | async-start | bytes 8388608 | tf_op jit(solution)/shard_map/all_to_all | solution.py:64
  27.3 60.0 %all-gather.2.cloned.1.call-start = ((), (), s32[]{:S(2)}) async-start(), calls=%async_computation.2 | async-start | bytes 6291456 | tf_op jit(solution)/shard_map/all_gather | solution.py:43
  90.5 2.0 %copy-start.1 = (bf16[32,128,512]{2,1,0:T(8,128)(2,1)}, bf16[32,128,512]{2,1,0:T(8,128)(2,1)S(1)}, u32[]{:S(2)}) copy-start(bf16[32,128,512]{2,1,0:T(8,128)(2,1)S(1)} %multiply_convert_fusion) | copy-start | bytes 12582916
  135.9 16.3 %all-to-all-start.1 = ((f32[2,256,512]{1,2,0:T(8,128)}), f32[2,256,512]{1,2,0:T(8,128)S(1)}, u32[]{:S(2)}, u32[]{:S(2)}) async-start(f32[2,256,512]{1,2,0:T(8,128)} %copy.43), calls=%async_computation.1 | async-start | bytes 2097152 | tf_op jit(solution)/shard_map/all_to_all | solution.py:68
Sparse Core Ops, SparseCore 0:
  29.7 57.5 all-gather.1
where the time goes:
time: 163 us; the launch traced here: 160 us
  waiting for transfers between devices  88.7 us (54%)
  local copies, waits for them, and re-layouts  26.7 us (16%)
  between operations  14.1 us (9%)
  starting transfers between devices  10.1 us (6%)
  matrix products  9.76 us (6%)
  other arithmetic  7.07 us (4%)
  blocking collectives  3.67 us (2%)
    all_gather x1, waiting for transfers between devices, shards(): piece_levels = lax.all_gather(level_blocks, 'inner', axis=0, tiled=True)  55.6 us
    all_to_all x1, waiting for transfers between devices, shards(): lax.all_to_all(term_blocks, ('outer', 'pair'), split_axis=1, concat_axis=...  26.7 us
    all_to_all x1, local copies, waits for them, and re-layouts, shards(): lax.all_to_all(term_blocks, ('outer', 'pair'), split_axis=1, concat_axis=...  11.1 us
    all_to_all x1, starting transfers between devices, shards(): lax.all_to_all(term_blocks, ('outer', 'pair'), split_axis=1, concat_axis=...  6.51 us
    all_to_all x1, waiting for transfers between devices, shards(): lax.all_to_all(first_sums, 'inner', split_axis=0, concat_axis=0, tiled=True)  5.71 us
    unnamed x11, local copies, waits for them, and re-layouts  5.4 us
    reshape x1, local copies, waits for them, and re-layouts, shards(): term_blocks = partial_value.reshape(inner_count, outer_count, -1, kv_width)  5.21 us
    dot_general x1, matrix products, shards(): lax.dot_general(grad_values, piece_weight, (((1,), (1,)), ((), ())), pref...  4.65 us
  transfers between devices with their start and end apart: 3, of which 3 were waited for; matrix products, arithmetic and copies ran while one was open for 7% of the time, Pallas kernels for 0%

commit v1 on v0

v1 whole, which is shorter than its diff:
```python
import functools
import math

import jax
import jax.numpy as jnp
from jax import lax
from jax.experimental import pallas as pl
from jax.experimental.pallas import tpu as pltpu
from jax.sharding import PartitionSpec as P

HD = 128
KVH = 4
GROUP = 4
TILE = 512
MESH = pl.DeviceIdType.MESH


def dot(a, b, dims):
    return lax.dot_general(a, b, (dims, ((), ())), preferred_element_type=jnp.float32)


def kernel(
    inner, outer, splits,
    tokens, queries, keys, grad_out, segments, levels, scales,
    attn_out, grad_tokens, grad_weight,
    weight, probs, tok_all, gv_all, part, pair_send, pair_recv, z_send, z_recv, acc,
    tok_s, tok_r, gv_s, gv_r, w_s, w_r, pair_s, pair_r, z_s, z_r,
):
    g = lax.axis_index("groups")
    x = lax.axis_index("inner")
    z = lax.axis_index("outer")
    c = lax.axis_index("pair")
    length = tokens.shape[1]
    shard = levels.shape[0]
    quarter = shard // 4
    piece = quarter // splits
    kv = levels.shape[1]
    rows = grad_weight.shape[0]
    per_tile = TILE // (2 * rows)
    tiles = shard // TILE

    x_to = [lax.rem(x + k, inner) for k in range(inner)]
    x_from = [lax.rem(x + inner - k, inner) for k in range(inner)]
    z_to = [lax.rem(z + k, outer) for k in range(outer)]
    mate = {"pair": 1 - c}
    across = {"groups": 1 - g}

    barrier = pltpu.get_barrier_semaphore()
    peers = [{"inner": x_to[k]} for k in range(1, inner)]
    peers += [{"outer": z_to[k]} for k in range(1, outer)]
    peers += [mate, across]
    for peer in peers:
        pl.semaphore_signal(barrier, inc=1, device_id=peer, device_id_type=MESH)
    pl.semaphore_wait(barrier, len(peers))

    def remote(src, dst, send, recv, peer):
        return pltpu.make_async_remote_copy(
            src_ref=src, dst_ref=dst, send_sem=send, recv_sem=recv,
            device_id=peer, device_id_type=MESH,
        )

    def aligned(value, unit):
        return pl.multiple_of(value, unit)

    if per_tile == 1:
        order = sorted(range(1, outer), key=lambda k: -min(k, outer - k)) + [0]
        tile_at = [z_to[k] for k in order]
    else:
        order = list(range(1, outer)) + [0]
        tile_at = list(range(tiles))

    def tok_copy(k, j):
        col = aligned(x_to[k] * shard + tile_at[j] * TILE, TILE)
        to = aligned(tile_at[j] * TILE, TILE)
        return remote(
            tokens.at[0, :, pl.ds(col, TILE)], tok_all.at[x, :, pl.ds(to, TILE)],
            tok_s.at[k - 1, j], tok_r.at[k - 1, j], {"inner": x_to[k]},
        )

    def gv_copy(k):
        return remote(
            gv_all.at[x], gv_all.at[x], gv_s.at[k - 1], gv_r.at[k - 1], {"inner": x_to[k]}
        )

    def w_copy(kind, k, n):
        owner = x if kind == 0 else x_from[k]
        group = 1 - g if kind == 3 else g
        row = aligned((group * 2 + c) * quarter + n * piece, piece)
        block = weight.at[owner, pl.ds(row, piece), :]
        peer = ({"inner": x_to[k]}, mate, across, mate)[kind]
        return remote(block, block, w_s.at[kind, k - 1, n], w_r.at[kind, k - 1, n], peer)

    half = max(1, tiles // 2)
    for j in range(half):
        for k in range(1, inner):
            tok_copy(k, j).start()

    def dequantize(q):
        blocks = quarter // 128
        lev = levels[pl.ds(aligned(q * quarter, quarter), quarter), :].astype(jnp.float32)
        for q_static in range(4):
            @pl.when(q == q_static)
            def _():
                sc = scales[q_static * blocks:(q_static + 1) * blocks, :].astype(jnp.float32)
                out = lev.reshape(blocks, 128, kv) * sc[:, None, :]
                weight[x, q_static * quarter:(q_static + 1) * quarter, :] = (
                    out.reshape(quarter, kv).astype(jnp.bfloat16)
                )

    seg = jnp.broadcast_to(segments[...].astype(jnp.float32), (length, length))
    pos_i = lax.broadcasted_iota(jnp.int32, (length, length), 0)
    pos_j = lax.broadcasted_iota(jnp.int32, (length, length), 1)
    allowed = (pos_j <= pos_i) & (seg == seg.T)
    for h in range(KVH):
        base = h * GROUP * HD
        key = keys[0, :, h * HD:(h + 1) * HD]
        query = jnp.concatenate(
            [queries[0, :, base + i * HD:base + (i + 1) * HD] for i in range(GROUP)], axis=0
        )
        cot = jnp.concatenate(
            [grad_out[0, :, base + i * HD:base + (i + 1) * HD] for i in range(GROUP)], axis=0
        )
        scores = dot(query, key, ((1,), (1,))) / math.sqrt(HD)
        scores = scores.reshape(GROUP, length, length)
        scores = jnp.where(allowed[None], scores, jnp.float32(-1e30))
        expo = jnp.exp(scores - jnp.max(scores, axis=-1, keepdims=True))
        p = (expo / jnp.sum(expo, axis=-1, keepdims=True)).astype(jnp.bfloat16)
        p = p.reshape(GROUP * length, length)
        probs[h] = p
        gv_all[x, :, h * HD:(h + 1) * HD] = dot(p, cot, ((0,), (0,))).astype(jnp.bfloat16)

    for k in range(1, inner):
        gv_copy(k).start()
    for j in range(half, tiles):
        for k in range(1, inner):
            tok_copy(k, j).start()
    mine = g * 2 + c
    dequantize(mine)
    for n in range(splits):
        for k in range(1, inner):
            w_copy(0, k, n).start()
    for k in range(1, 4):
        dequantize(lax.rem(mine + k, 4))

    tok_all[x] = tokens[0, :, pl.ds(aligned(x * shard, shard), shard)]
    gv_own = gv_all[x]

    def products(owner, first, count):
        w = weight[owner, pl.ds(first, count), :]
        col = aligned(owner * shard + first, 128)
        acc[...] += dot(tokens[0, :, pl.ds(col, count)], w, ((1,), (0,)))
        grad_tokens[0, :, pl.ds(col, count)] = dot(gv_own, w, ((1,), (1,))).astype(jnp.bfloat16)

    acc[...] = jnp.zeros_like(acc)
    for q in range(4):
        products(x, q * quarter, quarter)

    for k in range(1, inner):
        gv_copy(k).wait_recv()
    gv = gv_all[...].reshape(inner * length, kv)

    def pair_copy(j):
        block = pl.ds(tile_at[j] * per_tile, per_tile)
        return remote(
            pair_send.at[block], pair_recv.at[block], pair_s.at[j], pair_r.at[j], mate
        )

    def z_copy(k):
        return remote(
            z_send.at[z_to[k]], z_recv.at[k - 1], z_s.at[k - 1], z_r.at[k - 1],
            {"outer": z_to[k]},
        )

    def tile_sum(j):
        for k in range(1, inner):
            tok_copy(k, j).wait_recv()
        col = aligned(tile_at[j] * TILE, TILE)
        tok = tok_all[:, :, pl.ds(col, TILE)].reshape(inner * length, TILE)
        total = dot(tok, gv, ((0,), (0,))).reshape(per_tile, 2, rows, kv)
        block = pl.ds(tile_at[j] * per_tile, per_tile)
        part[block] = total
        pair_send[block] = part[block, 1 - c].astype(jnp.bfloat16)
        pair_copy(j).start()

    def send_along(k):
        to = z_to[k]
        total = part[to, c] + pair_recv[to].astype(jnp.float32)
        if k == 0:
            part[to, c] = total
        else:
            z_send[to] = total.astype(jnp.bfloat16)
            z_copy(k).start()

    for j in range(tiles):
        tile_sum(j)
        if per_tile == 1 and j > 0:
            pair_copy(j - 1).wait_recv()
            send_along(order[j - 1])
    if per_tile == 1:
        pair_copy(tiles - 1).wait_recv()
        send_along(order[tiles - 1])
    else:
        for j in range(tiles):
            pair_copy(j).wait_recv()
        for k in order:
            send_along(k)

    for n in range(splits):
        for k in range(1, inner):
            w_copy(0, k, n).wait_recv()
            w_copy(2, k, n).start()
            w_copy(1, k, n).start()
            products(x_from[k], aligned(mine * quarter + n * piece, piece), piece)
    other = (1 - g) * 2 + c
    for n in range(splits):
        for k in range(1, inner):
            w_copy(2, k, n).wait_recv()
            w_copy(3, k, n).start()
            products(x_from[k], aligned(other * quarter + n * piece, piece), piece)
            w_copy(1, k, n).wait_recv()
            products(x_from[k], aligned((g * 2 + 1 - c) * quarter + n * piece, piece), piece)
    for n in range(splits):
        for k in range(1, inner):
            w_copy(3, k, n).wait_recv()
            products(x_from[k], aligned(((1 - g) * 2 + 1 - c) * quarter + n * piece, piece), piece)

    values = acc[...].astype(jnp.bfloat16)
    for h in range(KVH):
        out = dot(probs[h], values[:, h * HD:(h + 1) * HD], ((1,), (0,))).astype(jnp.bfloat16)
        for i in range(GROUP):
            col = (h * GROUP + i) * HD
            attn_out[0, :, col:col + HD] = out[i * length:(i + 1) * length]

    total = part[z, c]
    for k in order[:-1]:
        z_copy(k).wait_recv()
        total += z_recv[k - 1].astype(jnp.float32)
    grad_weight[...] = total

    for k in range(1, inner):
        gv_copy(k).wait_send()
        for j in range(tiles):
            tok_copy(k, j).wait_send()
        for n in range(splits):
            for kind in range(4):
                w_copy(kind, k, n).wait_send()
    for j in range(tiles):
        pair_copy(j).wait_send()
    for k in range(1, outer):
        z_copy(k).wait_send()


def shards(inner, outer, tokens, queries, keys, grad_out, segment_ids, levels, scales):
    length, width = tokens.shape[1:]
    shard, kv = levels.shape
    rows = shard // (2 * outer)
    quarter = shard // 4
    splits = max(1, quarter // 256)
    tiles = shard // TILE
    vmem = pl.BlockSpec(memory_space=pltpu.VMEM)
    bf16 = jnp.bfloat16
    dma = pltpu.SemaphoreType.DMA
    return pl.pallas_call(
        functools.partial(kernel, inner, outer, splits),
        out_shape=(
            jax.ShapeDtypeStruct(queries.shape, bf16),
            jax.ShapeDtypeStruct(tokens.shape, bf16),
            jax.ShapeDtypeStruct((rows, kv), jnp.float32),
        ),
        in_specs=[vmem] * 7,
        out_specs=(vmem,) * 3,
        scratch_shapes=[
            pltpu.VMEM((inner, shard, kv), bf16),
            pltpu.VMEM((KVH, GROUP * length, length), bf16),
            pltpu.VMEM((inner, length, shard), bf16),
            pltpu.VMEM((inner, length, kv), bf16),
            pltpu.VMEM((outer, 2, rows, kv), jnp.float32),
            pltpu.VMEM((outer, rows, kv), bf16),
            pltpu.VMEM((outer, rows, kv), bf16),
            pltpu.VMEM((outer, rows, kv), bf16),
            pltpu.VMEM((outer - 1, rows, kv), bf16),
            pltpu.VMEM((length, kv), jnp.float32),
            dma((inner - 1, tiles)), dma((inner - 1, tiles)),
            dma((inner - 1,)), dma((inner - 1,)),
            dma((4, inner - 1, splits)), dma((4, inner - 1, splits)),
            dma((tiles,)), dma((tiles,)),
            dma((outer - 1,)), dma((outer - 1,)),
        ],
        compiler_params=pltpu.CompilerParams(
            collective_id=0, has_side_effects=True, vmem_limit_bytes=48 * 1024 * 1024
        ),
    )(tokens, queries, keys, grad_out, segment_ids, levels, scales)


def solution(mesh):
    spread = ("groups", "inner", "outer", "pair")
    return jax.shard_map(
        functools.partial(shards, mesh.shape["inner"], mesh.shape["outer"]),
        mesh=mesh,
        in_specs=(
            P(spread, None, None),
            P(spread, None, None),
            P(spread, None, None),
            P(spread, None, None),
            P(spread, None),
            P("inner", None),
            P("inner", None),
        ),
        out_specs=(P(spread, None, None), P(spread, None, None), P(spread, None)),
        check_vma=False,
    )
```

time: 163 us -> 52.1 us (0.32); the launches traced: 160 us -> 51.8 us
  waiting for transfers between devices: 88.7 us -> 0 us
  Pallas kernels: 0 us -> 43 us
  local copies, waits for them, and re-layouts: 26.7 us -> 8.13 us
  between operations: 14.1 us -> 0.66 us
  starting transfers between devices: 10.1 us -> 0 us
  matrix products: 9.76 us -> 0 us
  other arithmetic: 7.07 us -> 0 us
  blocking collectives: 3.67 us -> 0 us
    all_gather x1 -> x0, waiting for transfers between devices: 55.6 us -> none  [shards(): piece_levels = lax.all_gather(level_blocks, 'inner', axis=0, tiled=True)]
    pallas_call x0 -> x1, Pallas kernels: none -> 43 us  [shards(): pl.pallas_call(functools.partial(kernel, inner, outer, splits), out_shape...]
    all_to_all x2 -> x0, waiting for transfers between devices: 32.4 us -> none  [the longest x1 26.7 us: shards(): lax.all_to_all(term_blocks, ('outer', 'pair'), split_axis=1, concat_axis=...]
    all_to_all x1 -> x0, local copies, waits for them, and re-layouts: 11.1 us -> none  [shards(): lax.all_to_all(term_blocks, ('outer', 'pair'), split_axis=1, concat_axis=...]
    all_to_all x2 -> x0, starting transfers between devices: 10.1 us -> none  [the longest x1 6.51 us: shards(): lax.all_to_all(term_blocks, ('outer', 'pair'), split_axis=1, concat_axis=...]
    dot_general x5 -> x0, matrix products: 9.26 us -> none  [the longest x1 4.65 us: shards(): lax.dot_general(grad_values, piece_weight, (((1,), (1,)), ((), ())), pref...]
    reshape x1 -> x0, local copies, waits for them, and re-layouts: 5.21 us -> none  [shards(): term_blocks = partial_value.reshape(inner_count, outer_count, -1, kv_width)]
    all_gather x1 -> x0, blocking collectives: 3.67 us -> none  [shards(): piece_scales = lax.all_gather(scales, 'inner', axis=0, tiled=True)]
  transfers between devices with their start and end apart: 3 -> 0, of which waited for: 3 -> 0; matrix products, arithmetic and copies ran while one was open for 7% -> 0% of each run, Pallas kernels for 0% -> 0%
where the time goes in v1:
time: 52.1 us; the launch traced here: 51.8 us
  Pallas kernels  43 us (83%)
  local copies, waits for them, and re-layouts  8.13 us (16%)
  between operations  0.66 us (1%)
    pallas_call x1, Pallas kernels, shards(): pl.pallas_call(functools.partial(kernel, inner, outer, splits), out_shape...  43 us
    unnamed x15, local copies, waits for them, and re-layouts  8.13 us

profile of v1, /device:TPU:1, one launch (start us, length us, event | category | flops | bytes accessed | tf_op | source)
XLA Modules:
  0.0 51.8 jit_solution(13572698100563442819)
XLA Ops:
  0.6 0.0 copy-start
  0.6 1.2 %copy-done = bf16[1,128,4096]{2,1,0:T(8,128)(2,1)S(1)} copy-done((bf16[1,128,4096]{2,1,0:T(8,128)(2,1)S(1)}, bf16[1,128,4096]{2,1,0:T(8,128)(2,1)}, u32[]{:S(2)}) %copy-start) | copy-done | bytes 1048600
  1.9 0.0 copy-start.1
  1.9 1.0 %copy-done.1 = bf16[1,128,2048]{2,1,0:T(8,128)(2,1)S(1)} copy-done((bf16[1,128,2048]{2,1,0:T(8,128)(2,1)S(1)}, bf16[1,128,2048]{2,1,0:T(8,128)(2,1)}, u32[]{:S(2)}) %copy-start.1) | copy-done | bytes 524312
  2.9 0.0 copy-start.2
  2.9 1.0 %copy-done.2 = bf16[1,128,2048]{2,1,0:T(8,128)(2,1)S(1)} copy-done((bf16[1,128,2048]{2,1,0:T(8,128)(2,1)S(1)}, bf16[1,128,2048]{2,1,0:T(8,128)(2,1)}, u32[]{:S(2)}) %copy-start.2) | copy-done | bytes 524312
  3.9 0.0 copy-start.3
  3.9 0.9 %copy-done.3 = bf16[1,128,512]{2,1,0:T(8,128)(2,1)S(1)} copy-done((bf16[1,128,512]{2,1,0:T(8,128)(2,1)S(1)}, bf16[1,128,512]{2,1,0:T(8,128)(2,1)}, u32[]{:S(2)}) %copy-start.3) | copy-done | bytes 131096
  4.8 0.0 copy-start.4
  4.8 0.7 %copy-done.4 = bf16[16,512]{1,0:T(8,128)(2,1)S(1)} copy-done((bf16[16,512]{1,0:T(8,128)(2,1)S(1)}, bf16[16,512]{1,0:T(8,128)(2,1)}, u32[]{:S(2)}) %copy-start.4) | copy-done | bytes 16408
  5.6 0.0 copy-start.5
  5.6 0.7 %copy-done.5 = s32[1,128]{1,0:T(1,128)S(1)} copy-done((s32[1,128]{1,0:T(1,128)S(1)}, s32[1,128]{1,0:T(1,128)}, u32[]{:S(2)}) %copy-start.5) | copy-done | bytes 536
  6.2 43.0 %shard_map.94 = (bf16[1,128,2048]{2,1,0:T(8,128)(2,1)S(1)}, bf16[1,128,4096]{2,1,0:T(8,128)(2,1)S(1)}, f32[256,512]{1,0:T(8,128)S(1)}) custom-call(bf16[1,128,4096]{2,1,0:T(8,128)(2,1)S(1)} %copy-done, bf16[1,128,2048]{2,1,0:T(8,128)(2,1)S(1)} %copy-done.1, bf16[1,128,512]{2,1,0:T(8,128)(2,1)S(1)} %copy-done.3, bf16[1,128,2048]{2,1,0:T(8,128)(2,1)S(1)} %copy-done.2, ...), custom_call_target="tpu_custom_call" | custom-call | tf_op jit(solution)/shard_map/pallas_call | solution.py:263
  49.2 0.8 %copy.13 = bf16[1,128,2048]{2,1,0:T(8,128)(2,1)} copy(bf16[1,128,2048]{2,1,0:T(8,128)(2,1)S(1)} %get-tuple-element.6) | data formatting | bytes 1048576
  50.0 1.0 %copy.14 = bf16[1,128,4096]{2,1,0:T(8,128)(2,1)} copy(bf16[1,128,4096]{2,1,0:T(8,128)(2,1)S(1)} %get-tuple-element.7) | data formatting | bytes 2097152
  51.0 0.8 %copy.15 = f32[256,512]{1,0:T(8,128)} copy(f32[256,512]{1,0:T(8,128)S(1)} %get-tuple-element.8) | data formatting | bytes 1048576
Async XLA Ops:
  0.6 1.2 %copy-start = (bf16[1,128,4096]{2,1,0:T(8,128)(2,1)S(1)}, bf16[1,128,4096]{2,1,0:T(8,128)(2,1)}, u32[]{:S(2)}) copy-start(bf16[1,128,4096]{2,1,0:T(8,128)(2,1)} %tokens.1) | copy-start | bytes 3145732
  1.9 1.0 %copy-start.1 = (bf16[1,128,2048]{2,1,0:T(8,128)(2,1)S(1)}, bf16[1,128,2048]{2,1,0:T(8,128)(2,1)}, u32[]{:S(2)}) copy-start(bf16[1,128,2048]{2,1,0:T(8,128)(2,1)} %queries.1) | copy-start | bytes 1572868
  2.9 1.0 %copy-start.2 = (bf16[1,128,2048]{2,1,0:T(8,128)(2,1)S(1)}, bf16[1,128,2048]{2,1,0:T(8,128)(2,1)}, u32[]{:S(2)}) copy-start(bf16[1,128,2048]{2,1,0:T(8,128)(2,1)} %grad_out.1) | copy-start | bytes 1572868
  3.9 0.9 %copy-start.3 = (bf16[1,128,512]{2,1,0:T(8,128)(2,1)S(1)}, bf16[1,128,512]{2,1,0:T(8,128)(2,1)}, u32[]{:S(2)}) copy-start(bf16[1,128,512]{2,1,0:T(8,128)(2,1)} %keys.1) | copy-start | bytes 393220
  4.8 0.7 %copy-start.4 = (bf16[16,512]{1,0:T(8,128)(2,1)S(1)}, bf16[16,512]{1,0:T(8,128)(2,1)}, u32[]{:S(2)}) copy-start(bf16[16,512]{1,0:T(8,128)(2,1)} %scales.1) | copy-start | bytes 49156
  5.6 0.7 %copy-start.5 = (s32[1,128]{1,0:T(1,128)S(1)}, s32[1,128]{1,0:T(1,128)}, u32[]{:S(2)}) copy-start(s32[1,128]{1,0:T(1,128)} %segments.1) | copy-start | bytes 1540

commit v2 on v1

--- a/solution.py
+++ b/solution.py
@@ -21,8 +21,10 @@
 
 def kernel(
     inner, outer, splits,
-    tokens, queries, keys, grad_out, segments, levels, scales,
-    attn_out, grad_tokens, grad_weight,
+    tokens_hbm, queries_hbm, keys_hbm, grad_out_hbm, segments_hbm, levels_hbm, scales_hbm,
+    attn_hbm, grad_tokens_hbm, grad_weight_hbm,
+    tokens, queries, keys, grad_out, segments, levels, scales, in_sem,
+    attn_out, grad_tokens, grad_weight, out_sem, piece_sem,
     weight, probs, tok_all, gv_all, part, pair_send, pair_recv, z_send, z_recv, acc,
     tok_s, tok_r, gv_s, gv_r, w_s, w_r, pair_s, pair_r, z_s, z_r,
 ):
@@ -30,12 +32,12 @@
     x = lax.axis_index("inner")
     z = lax.axis_index("outer")
     c = lax.axis_index("pair")
-    length = tokens.shape[1]
-    shard = levels.shape[0]
+    length = tokens_hbm.shape[1]
+    shard = levels_hbm.shape[0]
     quarter = shard // 4
     piece = quarter // splits
-    kv = levels.shape[1]
-    rows = grad_weight.shape[0]
+    kv = levels_hbm.shape[1]
+    rows = grad_weight_hbm.shape[0]
     per_tile = TILE // (2 * rows)
     tiles = shard // TILE
 
@@ -44,6 +46,28 @@
     z_to = [lax.rem(z + k, outer) for k in range(outer)]
     mate = {"pair": 1 - c}
     across = {"groups": 1 - g}
+
+    own = pl.ds(pl.multiple_of(x * shard, shard), shard)
+    loads = [
+        (queries_hbm, queries), (keys_hbm, keys), (segments_hbm, segments), (grad_out_hbm, grad_out),
+        (levels_hbm, levels), (scales_hbm, scales), (tokens_hbm, tokens),
+        (tokens_hbm.at[0, :, own], tok_all.at[x]),
+    ]
+    loads = [pltpu.make_async_copy(a, b, in_sem.at[i]) for i, (a, b) in enumerate(loads)]
+    for load in loads:
+        load.start()
+
+    def piece_store(owner, row, index):
+        cols = pl.ds(pl.multiple_of(owner * shard + row, piece), piece)
+        return pltpu.make_async_copy(
+            grad_tokens.at[0, :, cols], grad_tokens_hbm.at[0, :, cols], piece_sem.at[index]
+        )
+
+    own_store = pltpu.make_async_copy(
+        grad_tokens.at[0, :, own], grad_tokens_hbm.at[0, :, own], out_sem.at[0]
+    )
+    attn_store = pltpu.make_async_copy(attn_out, attn_hbm, out_sem.at[1])
+    weight_store = pltpu.make_async_copy(grad_weight, grad_weight_hbm, out_sem.at[2])
 
     barrier = pltpu.get_barrier_semaphore()
     peers = [{"inner": x_to[k]} for k in range(1, inner)]
@@ -73,7 +97,7 @@
         col = aligned(x_to[k] * shard + tile_at[j] * TILE, TILE)
         to = aligned(tile_at[j] * TILE, TILE)
         return remote(
-            tokens.at[0, :, pl.ds(col, TILE)], tok_all.at[x, :, pl.ds(to, TILE)],
+            tokens_hbm.at[0, :, pl.ds(col, TILE)], tok_all.at[x, :, pl.ds(to, TILE)],
             tok_s.at[k - 1, j], tok_r.at[k - 1, j], {"inner": x_to[k]},
         )
 
@@ -107,6 +131,8 @@
                     out.reshape(quarter, kv).astype(jnp.bfloat16)
                 )
 
+    for load in loads[:4]:
+        load.wait()
     seg = jnp.broadcast_to(segments[...].astype(jnp.float32), (length, length))
     pos_i = lax.broadcasted_iota(jnp.int32, (length, length), 0)
     pos_j = lax.broadcasted_iota(jnp.int32, (length, length), 1)
@@ -135,6 +161,8 @@
         for k in range(1, inner):
             tok_copy(k, j).start()
     mine = g * 2 + c
+    for load in loads[4:]:
+        load.wait()
     dequantize(mine)
     for n in range(splits):
         for k in range(1, inner):
@@ -142,7 +170,6 @@
     for k in range(1, 4):
         dequantize(lax.rem(mine + k, 4))
 
-    tok_all[x] = tokens[0, :, pl.ds(aligned(x * shard, shard), shard)]
     gv_own = gv_all[x]
 
     def products(owner, first, count):
@@ -154,6 +181,7 @@
     acc[...] = jnp.zeros_like(acc)
     for q in range(4):
         products(x, q * quarter, quarter)
+    own_store.start()
 
     for k in range(1, inner):
         gv_copy(k).wait_recv()
@@ -205,24 +233,33 @@
         for k in order:
             send_along(k)
 
+    stores = []
+
+    def arrived(k, q, n):
+        row = aligned(q * quarter + n * piece, piece)
+        products(x_from[k], row, piece)
+        store = piece_store(x_from[k], row, len(stores))
+        store.start()
+        stores.append(store)
+
+    other = (1 - g) * 2 + c
     for n in range(splits):
         for k in range(1, inner):
             w_copy(0, k, n).wait_recv()
             w_copy(2, k, n).start()
             w_copy(1, k, n).start()
-            products(x_from[k], aligned(mine * quarter + n * piece, piece), piece)
-    other = (1 - g) * 2 + c
+            arrived(k, mine, n)
     for n in range(splits):
         for k in range(1, inner):
             w_copy(2, k, n).wait_recv()
             w_copy(3, k, n).start()
-            products(x_from[k], aligned(other * quarter + n * piece, piece), piece)
+            arrived(k, other, n)
             w_copy(1, k, n).wait_recv()
-            products(x_from[k], aligned((g * 2 + 1 - c) * quarter + n * piece, piece), piece)
+            arrived(k, g * 2 + 1 - c, n)
     for n in range(splits):
         for k in range(1, inner):
             w_copy(3, k, n).wait_recv()
-            products(x_from[k], aligned(((1 - g) * 2 + 1 - c) * quarter + n * piece, piece), piece)
+            arrived(k, (1 - g) * 2 + 1 - c, n)
 
     values = acc[...].astype(jnp.bfloat16)
     for h in range(KVH):
@@ -231,11 +268,13 @@
             col = (h * GROUP + i) * HD
             attn_out[0, :, col:col + HD] = out[i * length:(i + 1) * length]
 
+    attn_store.start()
     total = part[z, c]
     for k in order[:-1]:
         z_copy(k).wait_recv()
         total += z_recv[k - 1].astype(jnp.float32)
     grad_weight[...] = total
+    weight_store.start()
 
     for k in range(1, inner):
         gv_copy(k).wait_send()
@@ -248,6 +287,8 @@
         pair_copy(j).wait_send()
     for k in range(1, outer):
         z_copy(k).wait_send()
+    for store in [own_store, attn_store, weight_store] + stores:
+        store.wait()
 
 
 def shards(inner, outer, tokens, queries, keys, grad_out, segment_ids, levels, scales):
@@ -257,19 +298,32 @@
     quarter = shard // 4
     splits = max(1, quarter // 256)
     tiles = shard // TILE
-    vmem = pl.BlockSpec(memory_space=pltpu.VMEM)
+    hbm = pl.BlockSpec(memory_space=pltpu.HBM)
     bf16 = jnp.bfloat16
     dma = pltpu.SemaphoreType.DMA
-    return pl.pallas_call(
+    results = pl.pallas_call(
         functools.partial(kernel, inner, outer, splits),
         out_shape=(
             jax.ShapeDtypeStruct(queries.shape, bf16),
             jax.ShapeDtypeStruct(tokens.shape, bf16),
             jax.ShapeDtypeStruct((rows, kv), jnp.float32),
         ),
-        in_specs=[vmem] * 7,
-        out_specs=(vmem,) * 3,
+        in_specs=[hbm] * 7,
+        out_specs=(hbm,) * 3,
         scratch_shapes=[
+            pltpu.VMEM(tokens.shape, bf16),
+            pltpu.VMEM(queries.shape, bf16),
+            pltpu.VMEM(keys.shape, bf16),
+            pltpu.VMEM(grad_out.shape, bf16),
+            pltpu.VMEM(segment_ids.shape, jnp.int32),
+            pltpu.VMEM(levels.shape, bf16),
+            pltpu.VMEM(scales.shape, bf16),
+            dma((8,)),
+            pltpu.VMEM(queries.shape, bf16),
+            pltpu.VMEM(tokens.shape, bf16),
+            pltpu.VMEM((rows, kv), jnp.float32),
+            dma((3,)),
+            dma(((inner - 1) * 4 * splits,)),
             pltpu.VMEM((inner, shard, kv), bf16),
             pltpu.VMEM((KVH, GROUP * length, length), bf16),
             pltpu.VMEM((inner, length, shard), bf16),
@@ -287,9 +341,10 @@
             dma((outer - 1,)), dma((outer - 1,)),
         ],
         compiler_params=pltpu.CompilerParams(
-            collective_id=0, has_side_effects=True, vmem_limit_bytes=48 * 1024 * 1024
+            collective_id=0, has_side_effects=True, vmem_limit_bytes=60 * 1024 * 1024
         ),
     )(tokens, queries, keys, grad_out, segment_ids, levels, scales)
+    return results
 
 
 def solution(mesh):

time: 52.1 us -> 48.5 us (0.931)
  local copies, waits for them, and re-layouts: 8.13 us -> 5.02 us
    unnamed x15 -> x5, local copies, waits for them, and re-layouts: 8.13 us -> 5.02 us
where the time goes in v2:
time: 48.5 us; the launch traced here: 48.3 us
  Pallas kernels  42.7 us (88%)
  local copies, waits for them, and re-layouts  5.02 us (10%)
  between operations  0.65 us (1%)
    pallas_call x1, Pallas kernels, shards(): pl.pallas_call(functools.partial(kernel, inner, outer, splits), out_shape...  42.7 us
    unnamed x5, local copies, waits for them, and re-layouts  5.02 us

profile of v2, /device:TPU:1, one launch (start us, length us, event | category | flops | bytes accessed | tf_op | source)
XLA Modules:
  0.0 48.3 jit_solution(15851753550172001902)
XLA Ops:
  0.6 42.7 %shard_map.94 = (bf16[1,128,2048]{2,1,0:T(8,128)(2,1)}, bf16[1,128,4096]{2,1,0:T(8,128)(2,1)}, f32[256,512]{1,0:T(8,128)}) custom-call(bf16[1,128,4096]{2,1,0:T(8,128)(2,1)} %tokens_hbm.1, bf16[1,128,2048]{2,1,0:T(8,128)(2,1)} %queries_hbm.1, bf16[1,128,512]{2,1,0:T(8,128)(2,1)} %keys_hbm.1, bf16[1,128,2048]{2,1,0:T(8,128)(2,1)} %grad_out_hbm.1, ...), custom_call_target="tpu_custom_call" | custom-call | tf_op jit(solution)/shard_map/pallas_call | solution.py:304
  43.3 0.0 copy-start
  43.3 1.9 %copy.13 = bf16[1,128,2048]{2,1,0:T(8,128)(2,1)} copy(bf16[1,128,2048]{2,1,0:T(8,128)(2,1)} %get-tuple-element.6) | data formatting | bytes 1048576
  45.3 2.3 %copy.14 = bf16[1,128,4096]{2,1,0:T(8,128)(2,1)} copy(bf16[1,128,4096]{2,1,0:T(8,128)(2,1)} %get-tuple-element.7) | data formatting | bytes 2097152
  47.6 0.0 copy-done
  47.6 0.8 %copy.15 = f32[256,512]{1,0:T(8,128)} copy(f32[256,512]{1,0:T(8,128)S(1)} %copy-done) | data formatting | bytes 1048576
Async XLA Ops:
  43.3 4.2 %copy-start = (f32[256,512]{1,0:T(8,128)S(1)}, f32[256,512]{1,0:T(8,128)}, u32[]{:S(2)}) copy-start(f32[256,512]{1,0:T(8,128)} %get-tuple-element.8) | copy-start | bytes 1572868

commit v3 on v2

--- a/solution.py
+++ b/solution.py
@@ -12,6 +12,7 @@
 KVH = 4
 GROUP = 4
 TILE = 512
+SLICES = 2
 MESH = pl.DeviceIdType.MESH
 
 
@@ -114,7 +115,7 @@
         peer = ({"inner": x_to[k]}, mate, across, mate)[kind]
         return remote(block, block, w_s.at[kind, k - 1, n], w_r.at[kind, k - 1, n], peer)
 
-    half = max(1, tiles // 2)
+    half = min(1, tiles)
     for j in range(half):
         for k in range(1, inner):
             tok_copy(k, j).start()
@@ -167,9 +168,6 @@
     for n in range(splits):
         for k in range(1, inner):
             w_copy(0, k, n).start()
-    for k in range(1, 4):
-        dequantize(lax.rem(mine + k, 4))
-
     gv_own = gv_all[x]
 
     def products(owner, first, count):
@@ -177,11 +175,6 @@
         col = aligned(owner * shard + first, 128)
         acc[...] += dot(tokens[0, :, pl.ds(col, count)], w, ((1,), (0,)))
         grad_tokens[0, :, pl.ds(col, count)] = dot(gv_own, w, ((1,), (1,))).astype(jnp.bfloat16)
-
-    acc[...] = jnp.zeros_like(acc)
-    for q in range(4):
-        products(x, q * quarter, quarter)
-    own_store.start()
 
     for k in range(1, inner):
         gv_copy(k).wait_recv()
@@ -233,6 +226,14 @@
         for k in order:
             send_along(k)
 
+    for k in range(1, 4):
+        dequantize(lax.rem(mine + k, 4))
+
+    acc[...] = jnp.zeros_like(acc)
+    for q in range(4):
+        products(x, q * quarter, quarter)
+    own_store.start()
+
     stores = []
 
     def arrived(k, q, n):
@@ -288,6 +289,28 @@
     for k in range(1, outer):
         z_copy(k).wait_send()
     for store in [own_store, attn_store, weight_store] + stores:
+        store.wait()
+
+
+def store_kernel(copied, *refs):
+    sources, targets, held, sem = refs[:3], refs[3:6], refs[6:9], refs[9]
+
+    def copies(n):
+        i, part = copied[n]
+        width = held[i].shape[-1] // SLICES
+        at = (slice(None),) * (len(held[i].shape) - 1) + (pl.ds(part * width, width),)
+        return (
+            pltpu.make_async_copy(sources[i].at[at], held[i].at[at], sem.at[0, n]),
+            pltpu.make_async_copy(held[i].at[at], targets[i].at[at], sem.at[1, n]),
+        )
+
+    pairs = [copies(n) for n in range(len(copied))]
+    for load, _ in pairs:
+        load.start()
+    for load, store in pairs:
+        load.wait()
+        store.start()
+    for _, store in pairs:
         store.wait()
 
 
@@ -344,7 +367,16 @@
             collective_id=0, has_side_effects=True, vmem_limit_bytes=60 * 1024 * 1024
         ),
     )(tokens, queries, keys, grad_out, segment_ids, levels, scales)
-    return results
+    copied = [(i, part) for i, r in enumerate(results) for part in range(SLICES)]
+    return pl.pallas_call(
+        functools.partial(store_kernel, copied),
+        out_shape=[jax.ShapeDtypeStruct(r.shape, r.dtype) for r in results],
+        in_specs=[hbm] * 3,
+        out_specs=[hbm] * 3,
+        scratch_shapes=[pltpu.VMEM(r.shape, r.dtype) for r in results]
+        + [dma((2, len(copied)))],
+        compiler_params=pltpu.CompilerParams(vmem_limit_bytes=60 * 1024 * 1024),
+    )(*results)
 
 
 def solution(mesh):

time: 48.5 us -> 45.9 us (0.946)
  local copies, waits for them, and re-layouts: 5.02 us -> 0 us
  Pallas kernels: 42.7 us -> 45.1 us
    unnamed x5 -> x0, local copies, waits for them, and re-layouts: 5.02 us -> none
    pallas_call x0 -> x1, Pallas kernels: none -> 2.44 us  [shards(): pl.pallas_call(functools.partial(store_kernel, copied), out_shape=[jax.Sh...]
where the time goes in v3:
time: 45.9 us; the launch traced here: 45.8 us
  Pallas kernels  45.1 us (98%)
  between operations  0.64 us (1%)
    pallas_call x1, Pallas kernels, shards(): pl.pallas_call(functools.partial(kernel, inner, outer, splits), out_shape...  42.7 us
    pallas_call x1, Pallas kernels, shards(): pl.pallas_call(functools.partial(store_kernel, copied), out_shape=[jax.Sh...  2.44 us

profile of v3, /device:TPU:1, one launch (start us, length us, event | category | flops | bytes accessed | tf_op | source)
XLA Modules:
  0.0 45.8 jit_solution(5324427960145848169)
XLA Ops:
  0.6 42.7 %shard_map.94 = (bf16[1,128,2048]{2,1,0:T(8,128)(2,1)}, bf16[1,128,4096]{2,1,0:T(8,128)(2,1)}, f32[256,512]{1,0:T(8,128)}) custom-call(bf16[1,128,4096]{2,1,0:T(8,128)(2,1)} %tokens_hbm.1, bf16[1,128,2048]{2,1,0:T(8,128)(2,1)} %queries_hbm.1, bf16[1,128,512]{2,1,0:T(8,128)(2,1)} %keys_hbm.1, bf16[1,128,2048]{2,1,0:T(8,128)(2,1)} %grad_out_hbm.1, ...), custom_call_target="tpu_custom_call" | custom-call | tf_op jit(solution)/shard_map/pallas_call | solution.py:327
  43.3 2.4 %shard_map.95 = (bf16[1,128,2048]{2,1,0:T(8,128)(2,1)}, bf16[1,128,4096]{2,1,0:T(8,128)(2,1)}, f32[256,512]{1,0:T(8,128)}) custom-call(bf16[1,128,2048]{2,1,0:T(8,128)(2,1)} %get-tuple-element.6.refs_0_, bf16[1,128,4096]{2,1,0:T(8,128)(2,1)} %get-tuple-element.7.refs_1_, f32[256,512]{1,0:T(8,128)} %get-tuple-element.8.refs_2_), custom_call_target="tpu_custom_call" | custom-call | tf_op jit(solution)/shard_map/pallas_call | solution.py:371

commit v4 on v3

--- a/solution.py
+++ b/solution.py
@@ -226,14 +226,6 @@
         for k in order:
             send_along(k)
 
-    for k in range(1, 4):
-        dequantize(lax.rem(mine + k, 4))
-
-    acc[...] = jnp.zeros_like(acc)
-    for q in range(4):
-        products(x, q * quarter, quarter)
-    own_store.start()
-
     stores = []
 
     def arrived(k, q, n):
@@ -249,6 +241,16 @@
             w_copy(0, k, n).wait_recv()
             w_copy(2, k, n).start()
             w_copy(1, k, n).start()
+    for k in range(1, 4):
+        dequantize(lax.rem(mine + k, 4))
+
+    acc[...] = jnp.zeros_like(acc)
+    for q in range(4):
+        products(x, q * quarter, quarter)
+    own_store.start()
+
+    for n in range(splits):
+        for k in range(1, inner):
             arrived(k, mine, n)
     for n in range(splits):
         for k in range(1, inner):

time: 45.9 us -> 45.9 us (level)
  no operation moved by 1% of the time
where the time goes in v4:
time: 45.9 us; the launch traced here: 45.8 us
  Pallas kernels  45.1 us (98%)
  between operations  0.64 us (1%)
    pallas_call x1, Pallas kernels, shards(): pl.pallas_call(functools.partial(kernel, inner, outer, splits), out_shape...  42.7 us
    pallas_call x1, Pallas kernels, shards(): pl.pallas_call(functools.partial(store_kernel, copied), out_shape=[jax.Sh...  2.44 us

profile of v4, /device:TPU:1, one launch (start us, length us, event | category | flops | bytes accessed | tf_op | source)
XLA Modules:
  0.0 45.8 jit_solution(3032454644308842171)
XLA Ops:
  0.6 42.7 %shard_map.94 = (bf16[1,128,2048]{2,1,0:T(8,128)(2,1)}, bf16[1,128,4096]{2,1,0:T(8,128)(2,1)}, f32[256,512]{1,0:T(8,128)}) custom-call(bf16[1,128,4096]{2,1,0:T(8,128)(2,1)} %tokens_hbm.1, bf16[1,128,2048]{2,1,0:T(8,128)(2,1)} %queries_hbm.1, bf16[1,128,512]{2,1,0:T(8,128)(2,1)} %keys_hbm.1, bf16[1,128,2048]{2,1,0:T(8,128)(2,1)} %grad_out_hbm.1, ...), custom_call_target="tpu_custom_call" | custom-call | tf_op jit(solution)/shard_map/pallas_call | solution.py:329
  43.3 2.4 %shard_map.95 = (bf16[1,128,2048]{2,1,0:T(8,128)(2,1)}, bf16[1,128,4096]{2,1,0:T(8,128)(2,1)}, f32[256,512]{1,0:T(8,128)}) custom-call(bf16[1,128,2048]{2,1,0:T(8,128)(2,1)} %get-tuple-element.6.refs_0_, bf16[1,128,4096]{2,1,0:T(8,128)(2,1)} %get-tuple-element.7.refs_1_, f32[256,512]{1,0:T(8,128)} %get-tuple-element.8.refs_2_), custom_call_target="tpu_custom_call" | custom-call | tf_op jit(solution)/shard_map/pallas_call | solution.py:373
